TPU v7x, 32 devices: a whole 2x2x4 slice. The times are simulated.
32 devices in a mesh: tensor: 16 (over z, y, x), replica: 2 (over core).
Axes of the slice: x: 2, y: 2, z: 4, core: 2. Of those that a mesh axis runs over, the one named last changes fastest.
Arguments:
- amplitudes: bfloat16 [256, 64, 128], P('tensor'), may hold values from -6 to 6
- block_slot: int32 [256], replicated, may hold values from 0 to 255, each once
- integrals: bfloat16 [256, 16, 64, 64], P('tensor', 'replica'), may hold values from -0.1875 to 0.1875
- tile_cols: int32 [256, 16], P('tensor'), may hold values from 0 to 255, as said below
- irreps: int32 [256], replicated, may hold values from 0 to 7, as said below
Outputs:
- ladder: float32 [256, 64, 128], P('tensor', None, 'replica')
Inputs may be any that keep to these rules, and one draw needn't show every extreme that they name: `block_slot`: each block has one slot and each slot one block. `tile_cols`: the tiles of a row that name blocks of the row's own irrep name distinct blocks; other tiles may name any block of another irrep. `irreps`: each irrep labels exactly 32 blocks.
All inputs are finite; a program needn't handle non-finite values.
Results may differ from a plain program's by a relative error of at most 0.0003.
Values may be sent and summed in bfloat16 or wider, within the bound.
A program may use at most 128 MiB of HBM per device.

v0:
```python
import jax
import jax.numpy as jnp
from jax import lax
from jax.sharding import PartitionSpec as P


def local(amplitudes, block_slot, integrals, tile_cols, irreps):
    blocks = tile_cols.shape[0]
    rep_id = lax.axis_index("replica")
    rows_glob = lax.axis_index("tensor") * blocks + jnp.arange(blocks, dtype=jnp.int32)
    row_irrep = irreps[rows_glob]
    per_rep = integrals.shape[1]
    my_cols = lax.dynamic_slice_in_dim(tile_cols, rep_id * per_rep, per_rep, 1)
    whole = lax.all_gather(amplitudes, "tensor", axis=0, tiled=True)
    picked = whole[block_slot[my_cols]]
    allowed = (irreps[my_cols] == row_irrep[:, None]).astype(jnp.bfloat16)
    tiles = integrals * allowed[:, :, None, None]
    partial_sum = jnp.einsum("bnxy,bnyp->bxp", tiles, picked, preferred_element_type=jnp.float32)
    return lax.psum_scatter(partial_sum, "replica", scatter_dimension=2, tiled=True)


def solution(mesh):
    in_specs = (
        P("tensor", None, None),
        P(),
        P("tensor", "replica", None, None),
        P("tensor", None),
        P(),
    )
    out_specs = P("tensor", None, "replica")
    return jax.shard_map(local, mesh=mesh, in_specs=in_specs, out_specs=out_specs, check_vma=False)
```

profile of v0, /device:TPU:0, one launch (start us, length us, event | category | flops | bytes accessed | tf_op | source)
XLA Modules:
  0.0 111.8 jit_solution(6328258217071858476)
XLA Ops:
  6.5 0.0 copy-start
  6.5 0.0 all-gather.2.cloned.1.call-start
  6.5 0.7 all-gather.2.cloned.1.call-update
  7.3 0.0 reduce-scatter.4.cloned.1.call-start
  7.3 0.8 compare_select_fusion.1
  8.1 0.1 reshape.50
  8.2 0.0 copy-done
  8.2 0.7 gather_fusion.1
  8.9 0.0 copy-start.1
  8.9 1.3 %gather_fusion = s32[128]{0:T(128)S(1)} fusion(s32[256]{0:T(256)S(1)} %copy-done, s32[1024]{0:T(1024)S(1)} %pad_clamp_fusion.2), kind=kCustom, calls=%fused_computation | custom fusion | bytes 1536 | tf_op jit(solution)/shard_map/gather | solution.py:16
  10.2 0.0 copy-done.1
  10.2 1.3 %gather_fusion.2 = s32[128]{0:T(128)S(1)} fusion(s32[256]{0:T(256)S(1)} %copy-done.1, s32[1024]{0:T(1024)S(1)} %pad_clamp_fusion.2), kind=kCustom, calls=%fused_computation.2 | custom fusion | bytes 1536 | tf_op jit(solution)/shard_map/gather | solution.py:15
  11.5 0.1 reshape.49
  11.5 0.1 gather.17
  11.6 0.1 reshape.74
  11.7 0.1 compare_convert_fusion
  11.8 77.1 %all-gather.2.cloned.1.call-done = bf16[256,64,128]{2,1,0:T(8,128)(2,1)} async-done(((bf16[16,64,128]{2,1,0:T(8,128)(2,1)}), bf16[256,64,128]{2,1,0:T(8,128)(2,1)}) %all-gather.2.cloned.1.call-update) | async-done | bytes 4194320 | tf_op jit(solution)/shard_map/all_gather | solution.py:14
  88.9 3.1 %gather_fusion.3 = bf16[128,64,128]{2,1,0:T(8,128)(2,1)S(1)} fusion(bf16[256,64,128]{2,1,0:T(8,128)(2,1)} %all-gather.2.cloned.1.call-done, s32[1024]{0:T(1024)S(1)} %pad_clamp_fusion), kind=kCustom, calls=%fused_computation.3 | custom fusion | bytes 4194816 | tf_op jit(solution)/shard_map/gather | solution.py:15
  92.1 2.4 %fusion.2 = f32[16,64,128]{2,1,0:T(8,128)S(1)} fusion(bf16[16,8,64,128]{3,2,1,0:T(8,128)(2,1)S(1)} %bitcast.12, bf16[16,8,64,64]{3,2,1,0:T(8,128)(2,1)} %param.7, bf16[16,8]{1,0:T(8,128)(2,1)S(1)} %compare_convert_fusion), kind=kOutput, calls=%fused_computation.6 | convolution fusion | flops 134742016 | bytes 3670272 | tf_op jit(solution)/shard_map/bnxy,bnyp->bxp/dot_general | solution.py:18
  94.5 0.5 copy.7
  95.0 1.1 reshape.87
  96.1 0.0 reduce-scatter.4.cloned.1.call-update
  96.1 6.7 %reduce-scatter.4.cloned.1.call-done = f32[64,1024]{1,0:T(8,128)} async-done(((f32[128,1024]{1,0:T(8,128)}), f32[64,1024]{1,0:T(8,128)}) %reduce-scatter.4.cloned.1.call-update) | async-done | bytes 262160
  102.8 1.1 reshape.88
  103.9 1.1 copy.8
  (5 shorter events, 0.0 us)
Async XLA Ops:
  6.5 1.7 %copy-start = (s32[256]{0:T(256)S(1)}, s32[256]{0:T(256)}, u32[]{:S(2)}) copy-start(s32[256]{0:T(256)} %param.9) | copy-start | bytes 3076
  6.5 82.4 %all-gather.2.cloned.1.call-start = ((), (), s32[]{:S(2)}) async-start(), calls=%async_computation.1 | async-start | bytes 4456448 | tf_op jit(solution)/shard_map/all_gather | solution.py:14
  7.3 95.5 %reduce-scatter.4.cloned.1.call-start = ((), (), s32[]{:S(2)}) async-start(), calls=%async_computation.2 | async-start | bytes 786432
  8.9 1.3 %copy-start.1 = (s32[256]{0:T(256)S(1)}, s32[256]{0:T(256)}, u32[]{:S(2)}) copy-start(s32[256]{0:T(256)} %param.6) | copy-start | bytes 3076
Sparse Core Ops, SparseCore 0:
  10.1 78.7 all-gather.1
  96.2 6.5 reduce-scatter.3
where the time goes:
time: 112 us
  waiting for transfers between devices  84.5 us (75%)
  between operations  13.5 us (12%)
  local copies, waits for them, and re-layouts  10.4 us (9%)
  matrix products  2.36 us (2%)
    all_gather x1, waiting for transfers between devices, local(): whole = lax.all_gather(amplitudes, 'tensor', axis=0, tiled=True)  77.1 us
    unnamed x3, waiting for transfers between devices  7.43 us
    gather x3, local copies, waits for them, and re-layouts, local(): picked = whole[block_slot[my_cols]]  4.48 us
    unnamed x8, local copies, waits for them, and re-layouts  3.75 us
    dot_general x1, matrix products, local(): jnp.einsum('bnxy,bnyp->bxp', tiles, picked, preferred_element_type=jnp.fl...  2.36 us
  transfers between devices with their start and end apart: 2, of which 2 were waited for; matrix products, arithmetic and copies ran while one was open for 4% of the time, Pallas kernels for 0%

commit v1 on v0

v1 whole, which is shorter than its diff:
```python
import functools

import jax
import jax.numpy as jnp
from jax import lax
from jax.experimental import pallas as pl
from jax.experimental.pallas import tpu as pltpu
from jax.sharding import PartitionSpec as P

MESH = pl.DeviceIdType.MESH
ORDERS = ("yzx", "xzy")
X, Y, UP, DOWN = range(4)


def kernel(
    tensor, replica,
    slot_ref, cols_ref, irreps_ref, amp_hbm, tiles_hbm, out_ref,
    amps, tiles, lhs, index, outgo, income,
    local_sem, send_sem, recv_sem, pass_sem, got_sem, sum_send, sum_recv,
):
    layers = tensor // 4
    blocks = amp_hbm.shape[0]
    part = blocks // replica
    chunk = part // len(ORDERS)
    rows, per_rep = tiles.shape[0], tiles.shape[1]
    width = out_ref.shape[2]
    groups, wide = lhs.shape[1], per_rep // lhs.shape[1]
    zero_block = tensor * blocks
    t, r = lax.axis_index("tensor"), lax.axis_index("replica")
    z, y, x = t // 4, (t // 2) % 2, t % 2

    own = pltpu.make_async_copy(amp_hbm, amps.at[pl.ds(t * blocks, blocks)], local_sem.at[0])
    own.start()
    load_tiles = pltpu.make_async_copy(tiles_hbm, tiles, local_sem.at[1])
    load_tiles.start()

    target = {X: t + 1 - 2 * x, Y: t + 2 - 4 * y, UP: t + 4, DOWN: t - 4}
    exists = {X: None, Y: None, UP: z < layers - 1, DOWN: z > 0}

    def when(condition, body):
        if condition is None:
            body()
        else:
            pl.when(condition)(body)

    def both(a, b):
        return b if a is None else a if b is None else a & b

    barrier = pltpu.get_barrier_semaphore()

    def greet(device):
        pl.semaphore_signal(barrier, inc=1, device_id=device, device_id_type=MESH)

    for way in (X, Y, UP, DOWN):
        when(exists[way], functools.partial(greet, {"tensor": target[way], "replica": r}))
    for j in range(1, replica):
        greet({"tensor": t, "replica": (r + j) % replica})
    ends = (z == 0).astype(jnp.int32) + (z == layers - 1).astype(jnp.int32)
    pl.semaphore_wait(barrier, 4 - ends + replica - 1)

    def place(source, owner, flow):
        return amps.at[pl.ds(source * blocks + owner * part + flow * chunk, chunk)]

    def hop(flow, source, way):
        return pltpu.make_async_remote_copy(
            src_ref=place(source, r, flow), dst_ref=place(source, r, flow),
            send_sem=send_sem.at[flow, source, way], recv_sem=recv_sem.at[flow, source],
            device_id={"tensor": jnp.clip(target[way], 0, tensor - 1), "replica": r}, device_id_type=MESH,
        )

    def handover(flow, source, j):
        return pltpu.make_async_remote_copy(
            src_ref=place(source, r, flow), dst_ref=place(source, r, flow),
            send_sem=pass_sem.at[j - 1, flow, source], recv_sem=got_sem.at[j - 1, flow, source],
            device_id={"tensor": t, "replica": (r + j) % replica}, device_id_type=MESH,
        )

    def ways(flow, dx, dy, dz):
        order = ORDERS[flow]
        moved = {"x": dx, "y": dy, "z": dz}
        last = max([i for i, axis in enumerate(order) if moved[axis]], default=-1)
        found = []
        if last >= 0 and order[last] == "z":
            found.append(UP if dz > 0 else DOWN)
        for axis in order[last + 1:]:
            found += {"x": [X], "y": [Y], "z": [UP, DOWN]}[axis]
        return found

    def visit(action):
        def ring(k, carry):
            for flow in range(len(ORDERS)):
                for dx, dy in ((0, 0), (1, 0), (0, 1), (1, 1)):
                    d = k - dx - dy
                    base = t + dx * (1 - 2 * x) + dy * (2 - 4 * y)
                    if dx or dy:
                        action(d == 0, flow, base, ways(flow, dx, dy, 0))
                    for dz in (1, -1):
                        inside = (d >= 1) & ((d <= z) if dz > 0 else (d <= layers - 1 - z))
                        action(inside, flow, base - 4 * dz * d, ways(flow, dx, dy, dz))
            return carry

        lax.fori_loop(1, layers + 2, ring, 0)

    own.wait()
    for flow in range(len(ORDERS)):
        for way in ways(flow, 0, 0, 0):
            when(exists[way], lambda flow=flow, way=way: hop(flow, t, way).start())

    amps[zero_block] = jnp.zeros(amps.shape[1:], amps.dtype)
    load_tiles.wait()

    def pack(b, carry):
        for g in range(groups):
            lhs[b, g] = jnp.concatenate([tiles[b, g * wide + i] for i in range(wide)], axis=1)
        for n in range(per_rep):
            col = cols_ref[b, r * per_rep + n]
            same = irreps_ref[col] == irreps_ref[t * rows + b]
            index[b * per_rep + n] = jnp.where(same, slot_ref[col], zero_block)
        return carry

    lax.fori_loop(0, rows, pack, 0)

    def forward(condition, flow, source, onward):
        @pl.when(condition)
        def _():
            hop(flow, source, X).wait_recv()
            for way in onward:
                when(exists[way], lambda way=way: hop(flow, source, way).start())
            for j in range(1, replica):
                handover(flow, source, j).start()

    visit(forward)

    def arrived(condition, flow, source, onward):
        @pl.when(condition)
        def _():
            for j in range(1, replica):
                handover(flow, source, j).wait_recv()

    def got(source, carry):
        @pl.when(source != t)
        def _():
            for flow in range(len(ORDERS)):
                for j in range(1, replica):
                    pltpu.make_async_remote_copy(
                        src_ref=place(source, (r + replica - j) % replica, flow),
                        dst_ref=place(source, (r + replica - j) % replica, flow),
                        send_sem=pass_sem.at[j - 1, flow, source], recv_sem=got_sem.at[j - 1, flow, source],
                        device_id={"tensor": t, "replica": (r + j) % replica}, device_id_type=MESH,
                    ).wait_recv()
        return carry

    lax.fori_loop(0, tensor, got, 0)

    packs = rows // replica

    def sums(q, j):
        return pltpu.make_async_remote_copy(
            src_ref=outgo.at[j, q], dst_ref=income.at[j - 1, q],
            send_sem=sum_send.at[j - 1, q], recv_sem=sum_recv.at[j - 1, q],
            device_id={"tensor": t, "replica": (r + j) % replica}, device_id_type=MESH,
        )

    for q in range(packs):
        turned = []
        for i in range(replica):
            b = q * replica + i
            total = None
            for g in range(groups):
                rhs = jnp.concatenate(
                    [amps[index[b * per_rep + g * wide + n]] for n in range(wide)], axis=0
                )
                term = jnp.dot(lhs[b, g], rhs, preferred_element_type=jnp.float32)
                total = term if total is None else total + term
            turned.append(pltpu.roll(total, (replica - r) % replica * width, 1))
        for j in range(replica):
            outgo[j, q] = jnp.concatenate([v[:, j * width:(j + 1) * width] for v in turned], axis=1)
        for j in range(1, replica):
            sums(q, j).start()

    for q in range(packs):
        total = outgo[0, q]
        for j in range(1, replica):
            sums(q, j).wait_recv()
            total = total + income[j - 1, q]
        for i in range(replica):
            out_ref[q * replica + i] = total[:, i * width:(i + 1) * width]

    for flow in range(len(ORDERS)):
        for way in ways(flow, 0, 0, 0):
            when(exists[way], lambda flow=flow, way=way: hop(flow, t, way).wait_send())

    def sent(condition, flow, source, onward):
        @pl.when(condition)
        def _():
            for way in onward:
                when(exists[way], lambda way=way: hop(flow, source, way).wait_send())
            for j in range(1, replica):
                handover(flow, source, j).wait_send()

    visit(sent)
    for q in range(packs):
        for j in range(1, replica):
            sums(q, j).wait_send()


def solution(mesh):
    tensor, replica = mesh.shape["tensor"], mesh.shape["replica"]

    def local(amplitudes, block_slot, integrals, tile_cols, irreps):
        blocks, tile, occ = amplitudes.shape
        rows, per_rep = integrals.shape[:2]
        wide = max(w for w in (4, 2, 1) if per_rep % w == 0)
        groups = per_rep // wide
        packs = rows // replica
        flows = len(ORDERS)
        smem = pl.BlockSpec(memory_space=pltpu.SMEM)
        hbm = pl.BlockSpec(memory_space=pl.ANY)
        dma = pltpu.SemaphoreType.DMA
        others = max(replica - 1, 1)
        return pl.pallas_call(
            functools.partial(kernel, tensor, replica),
            out_shape=jax.ShapeDtypeStruct((rows, tile, occ // replica), jnp.float32),
            in_specs=[smem, smem, smem, hbm, hbm],
            out_specs=pl.BlockSpec(memory_space=pltpu.VMEM),
            scratch_shapes=[
                pltpu.VMEM((tensor * blocks + 1, tile, occ), amplitudes.dtype),
                pltpu.VMEM(integrals.shape, integrals.dtype),
                pltpu.VMEM((rows, groups, tile, wide * tile), integrals.dtype),
                pltpu.SMEM((rows * per_rep,), jnp.int32),
                pltpu.VMEM((replica, packs, tile, occ), jnp.float32),
                pltpu.VMEM((others, packs, tile, occ), jnp.float32),
                dma((2,)),
                dma((flows, tensor, 4)),
                dma((flows, tensor)),
                dma((others, flows, tensor)),
                dma((others, flows, tensor)),
                dma((others, packs)),
                dma((others, packs)),
            ],
            compiler_params=pltpu.CompilerParams(
                collective_id=0, has_side_effects=True, vmem_limit_bytes=48 << 20
            ),
            cost_estimate=pl.CostEstimate(
                flops=2 * rows * per_rep * tile * tile * occ, bytes_accessed=4 << 20, transcendentals=0
            ),
        )(block_slot, tile_cols, irreps, amplitudes, integrals)

    in_specs = (
        P("tensor", None, None),
        P(),
        P("tensor", "replica", None, None),
        P("tensor", None),
        P(),
    )
    out_specs = P("tensor", None, "replica")
    return jax.shard_map(local, mesh=mesh, in_specs=in_specs, out_specs=out_specs, check_vma=False)
```

time: 112 us -> 40.2 us (0.36)
  waiting for transfers between devices: 84.5 us -> 0 us
  Pallas kernels: 0 us -> 34.6 us
  between operations: 13.5 us -> 0.01 us
  local copies, waits for them, and re-layouts: 10.4 us -> 5.39 us
  matrix products: 2.36 us -> 0 us
    all_gather x1 -> x0, waiting for transfers between devices: 77.1 us -> none  [local(): whole = lax.all_gather(amplitudes, 'tensor', axis=0, tiled=True)]
    pallas_call x0 -> x1, Pallas kernels: none -> 34.6 us  [local(): pl.pallas_call(functools.partial(kernel, tensor, replica), out_shape=jax....]
    unnamed x3 -> x0, waiting for transfers between devices: 7.43 us -> none
    gather x6 -> x0, local copies, waits for them, and re-layouts: 6.5 us -> none  [the longest x3 4.48 us: local(): picked = whole[block_slot[my_cols]]]
    dot_general x1 -> x0, matrix products: 2.36 us -> none  [local(): jnp.einsum('bnxy,bnyp->bxp', tiles, picked, preferred_element_type=jnp.fl...]
    unnamed x8 -> x11, local copies, waits for them, and re-layouts: 3.75 us -> 5.39 us
  transfers between devices with their start and end apart: 2 -> 0, of which waited for: 2 -> 0; matrix products, arithmetic and copies ran while one was open for 4% -> 0% of each run, Pallas kernels for 0% -> 0%
where the time goes in v1:
time: 40.2 us; the launch traced here: 40 us
  Pallas kernels  34.6 us (86%)
  local copies, waits for them, and re-layouts  5.39 us (13%)
    pallas_call x1, Pallas kernels, local(): pl.pallas_call(functools.partial(kernel, tensor, replica), out_shape=jax....  34.6 us
    unnamed x11, local copies, waits for them, and re-layouts  5.39 us

profile of v1, /device:TPU:0, one launch (start us, length us, event | category | flops | bytes accessed | tf_op | source)
XLA Modules:
  0.0 40.0 jit_solution(18333896665910056405)
XLA Ops:
  0.0 0.0 copy-start
  0.0 1.6 %copy-done = bf16[16,8,64,64]{3,2,1,0:T(8,128)(2,1)S(1)} copy-done((bf16[16,8,64,64]{3,2,1,0:T(8,128)(2,1)S(1)}, bf16[16,8,64,64]{3,2,1,0:T(8,128)(2,1)}, u32[]{:S(2)}) %copy-start) | copy-done | bytes 1048600
  1.6 0.0 copy-start.1
  1.6 0.9 %copy-done.1 = bf16[16,64,128]{2,1,0:T(8,128)(2,1)S(1)} copy-done((bf16[16,64,128]{2,1,0:T(8,128)(2,1)S(1)}, bf16[16,64,128]{2,1,0:T(8,128)(2,1)}, u32[]{:S(2)}) %copy-start.1) | copy-done | bytes 262168
  2.5 0.0 copy-start.2
  2.5 0.7 %copy-done.2 = s32[16,16]{1,0:T(8,128)S(1)} copy-done((s32[16,16]{1,0:T(8,128)S(1)}, s32[16,16]{1,0:T(8,128)}, u32[]{:S(2)}) %copy-start.2) | copy-done | bytes 1048
  3.2 0.0 copy-start.3
  3.2 0.7 %copy-done.3 = s32[256]{0:T(256)S(1)} copy-done((s32[256]{0:T(256)S(1)}, s32[256]{0:T(256)}, u32[]{:S(2)}) %copy-start.3) | copy-done | bytes 1048
  3.9 0.0 copy-start.4
  3.9 0.7 %copy-done.4 = s32[256]{0:T(256)S(1)} copy-done((s32[256]{0:T(256)S(1)}, s32[256]{0:T(256)}, u32[]{:S(2)}) %copy-start.4) | copy-done | bytes 1048
  4.6 34.6 %shard_map.55 = f32[16,64,64]{2,1,0:T(8,128)S(1)} custom-call(s32[256]{0:T(256)S(1)} %copy-done.3, s32[16,16]{1,0:T(8,128)S(1)} %copy-done.2, s32[256]{0:T(256)S(1)} %copy-done.4, bf16[16,64,128]{2,1,0:T(8,128)(2,1)S(1)} %copy-done.1, bf16[16,8,64,64]{3,2,1,0:T(8,128)(2,1)S(1)} %copy-done), custom_call_target="tpu_custom_call" | custom-call | flops 134217728 | bytes 4194304 | tf_op jit(solution)/shard_map/pallas_call | solution.py:221
  39.2 0.8 %copy.7 = f32[16,64,64]{2,1,0:T(8,128)} copy(f32[16,64,64]{2,1,0:T(8,128)S(1)} %shard_map.55) | data formatting | bytes 524288
Async XLA Ops:
  0.0 1.6 %copy-start = (bf16[16,8,64,64]{3,2,1,0:T(8,128)(2,1)S(1)}, bf16[16,8,64,64]{3,2,1,0:T(8,128)(2,1)}, u32[]{:S(2)}) copy-start(bf16[16,8,64,64]{3,2,1,0:T(8,128)(2,1)} %tiles_hbm.1) | copy-start | bytes 3145732
  1.6 0.9 %copy-start.1 = (bf16[16,64,128]{2,1,0:T(8,128)(2,1)S(1)}, bf16[16,64,128]{2,1,0:T(8,128)(2,1)}, u32[]{:S(2)}) copy-start(bf16[16,64,128]{2,1,0:T(8,128)(2,1)} %amp_hbm.1) | copy-start | bytes 786436
  2.5 0.7 %copy-start.2 = (s32[16,16]{1,0:T(8,128)S(1)}, s32[16,16]{1,0:T(8,128)}, u32[]{:S(2)}) copy-start(s32[16,16]{1,0:T(8,128)} %cols_ref.1) | copy-start | bytes 3076
  3.2 0.7 %copy-start.3 = (s32[256]{0:T(256)S(1)}, s32[256]{0:T(256)}, u32[]{:S(2)}) copy-start(s32[256]{0:T(256)} %slot_ref.1) | copy-start | bytes 3076
  3.9 0.7 %copy-start.4 = (s32[256]{0:T(256)S(1)}, s32[256]{0:T(256)}, u32[]{:S(2)}) copy-start(s32[256]{0:T(256)} %irreps_ref.1) | copy-start | bytes 3076

commit v2 on v1

--- a/solution.py
+++ b/solution.py
@@ -8,20 +8,33 @@
 from jax.sharding import PartitionSpec as P
 
 MESH = pl.DeviceIdType.MESH
-ORDERS = ("yzx", "xzy")
 X, Y, UP, DOWN = range(4)
+
+
+def split(part):
+    plan = (("zyx", 1), ("zxy", 1))
+    total = sum(n for _, n in plan)
+    if part % total:
+        plan, total = (("yzx", 1), ("xzy", 1)), 2
+    if part % total:
+        plan, total = (("yzx", 1),), 1
+    flows, first = [], 0
+    for order, n in plan:
+        flows.append((order, first, n * part // total))
+        first += n * part // total
+    return flows
 
 
 def kernel(
     tensor, replica,
-    slot_ref, cols_ref, irreps_ref, amp_hbm, tiles_hbm, out_ref,
-    amps, tiles, lhs, index, outgo, income,
+    slot_hbm, cols_hbm, irreps_hbm, amp_hbm, tiles_hbm, out_ref,
+    amps, tiles, lhs, index, slot_ref, cols_ref, irreps_ref, outgo, income,
     local_sem, send_sem, recv_sem, pass_sem, got_sem, sum_send, sum_recv,
 ):
     layers = tensor // 4
     blocks = amp_hbm.shape[0]
     part = blocks // replica
-    chunk = part // len(ORDERS)
+    flows = split(part)
     rows, per_rep = tiles.shape[0], tiles.shape[1]
     width = out_ref.shape[2]
     groups, wide = lhs.shape[1], per_rep // lhs.shape[1]
@@ -33,6 +46,12 @@
     own.start()
     load_tiles = pltpu.make_async_copy(tiles_hbm, tiles, local_sem.at[1])
     load_tiles.start()
+    small = [
+        pltpu.make_async_copy(src, dst, local_sem.at[2 + i])
+        for i, (src, dst) in enumerate(((slot_hbm, slot_ref), (cols_hbm, cols_ref), (irreps_hbm, irreps_ref)))
+    ]
+    for copy in small:
+        copy.start()
 
     target = {X: t + 1 - 2 * x, Y: t + 2 - 4 * y, UP: t + 4, DOWN: t - 4}
     exists = {X: None, Y: None, UP: z < layers - 1, DOWN: z > 0}
@@ -59,7 +78,7 @@
     pl.semaphore_wait(barrier, 4 - ends + replica - 1)
 
     def place(source, owner, flow):
-        return amps.at[pl.ds(source * blocks + owner * part + flow * chunk, chunk)]
+        return amps.at[pl.ds(source * blocks + owner * part + flows[flow][1], flows[flow][2])]
 
     def hop(flow, source, way):
         return pltpu.make_async_remote_copy(
@@ -76,7 +95,7 @@
         )
 
     def ways(flow, dx, dy, dz):
-        order = ORDERS[flow]
+        order = flows[flow][0]
         moved = {"x": dx, "y": dy, "z": dz}
         last = max([i for i, axis in enumerate(order) if moved[axis]], default=-1)
         found = []
@@ -88,7 +107,7 @@
 
     def visit(action):
         def ring(k, carry):
-            for flow in range(len(ORDERS)):
+            for flow in range(len(flows)):
                 for dx, dy in ((0, 0), (1, 0), (0, 1), (1, 1)):
                     d = k - dx - dy
                     base = t + dx * (1 - 2 * x) + dy * (2 - 4 * y)
@@ -102,12 +121,14 @@
         lax.fori_loop(1, layers + 2, ring, 0)
 
     own.wait()
-    for flow in range(len(ORDERS)):
+    for flow in range(len(flows)):
         for way in ways(flow, 0, 0, 0):
             when(exists[way], lambda flow=flow, way=way: hop(flow, t, way).start())
 
     amps[zero_block] = jnp.zeros(amps.shape[1:], amps.dtype)
     load_tiles.wait()
+    for copy in small:
+        copy.wait()
 
     def pack(b, carry):
         for g in range(groups):
@@ -131,16 +152,10 @@
 
     visit(forward)
 
-    def arrived(condition, flow, source, onward):
-        @pl.when(condition)
-        def _():
-            for j in range(1, replica):
-                handover(flow, source, j).wait_recv()
-
     def got(source, carry):
         @pl.when(source != t)
         def _():
-            for flow in range(len(ORDERS)):
+            for flow in range(len(flows)):
                 for j in range(1, replica):
                     pltpu.make_async_remote_copy(
                         src_ref=place(source, (r + replica - j) % replica, flow),
@@ -186,7 +201,7 @@
         for i in range(replica):
             out_ref[q * replica + i] = total[:, i * width:(i + 1) * width]
 
-    for flow in range(len(ORDERS)):
+    for flow in range(len(flows)):
         for way in ways(flow, 0, 0, 0):
             when(exists[way], lambda flow=flow, way=way: hop(flow, t, way).wait_send())
 
@@ -213,24 +228,26 @@
         wide = max(w for w in (4, 2, 1) if per_rep % w == 0)
         groups = per_rep // wide
         packs = rows // replica
-        flows = len(ORDERS)
-        smem = pl.BlockSpec(memory_space=pltpu.SMEM)
-        hbm = pl.BlockSpec(memory_space=pl.ANY)
+        flows = len(split(blocks // replica))
+        hbm = pl.BlockSpec(memory_space=pltpu.HBM)
         dma = pltpu.SemaphoreType.DMA
         others = max(replica - 1, 1)
         return pl.pallas_call(
             functools.partial(kernel, tensor, replica),
             out_shape=jax.ShapeDtypeStruct((rows, tile, occ // replica), jnp.float32),
-            in_specs=[smem, smem, smem, hbm, hbm],
+            in_specs=[hbm] * 5,
             out_specs=pl.BlockSpec(memory_space=pltpu.VMEM),
             scratch_shapes=[
                 pltpu.VMEM((tensor * blocks + 1, tile, occ), amplitudes.dtype),
                 pltpu.VMEM(integrals.shape, integrals.dtype),
                 pltpu.VMEM((rows, groups, tile, wide * tile), integrals.dtype),
                 pltpu.SMEM((rows * per_rep,), jnp.int32),
+                pltpu.SMEM(block_slot.shape, jnp.int32),
+                pltpu.SMEM(tile_cols.shape, jnp.int32),
+                pltpu.SMEM(irreps.shape, jnp.int32),
                 pltpu.VMEM((replica, packs, tile, occ), jnp.float32),
                 pltpu.VMEM((others, packs, tile, occ), jnp.float32),
-                dma((2,)),
+                dma((5,)),
                 dma((flows, tensor, 4)),
                 dma((flows, tensor)),
                 dma((others, flows, tensor)),
@@ -239,7 +256,7 @@
                 dma((others, packs)),
             ],
             compiler_params=pltpu.CompilerParams(
-                collective_id=0, has_side_effects=True, vmem_limit_bytes=48 << 20
+                collective_id=0, has_side_effects=True, vmem_limit_bytes=60 << 20
             ),
             cost_estimate=pl.CostEstimate(
                 flops=2 * rows * per_rep * tile * tile * occ, bytes_accessed=4 << 20, transcendentals=0

time: 40.2 us -> 35.3 us (0.88)
  local copies, waits for them, and re-layouts: 5.39 us -> 1.89 us
  Pallas kernels: 34.6 us -> 33.2 us
    unnamed x11 -> x1, local copies, waits for them, and re-layouts: 5.39 us -> 1.89 us
    pallas_call x1, Pallas kernels: 34.6 us -> 33.2 us  [local(): pl.pallas_call(functools.partial(kernel, tensor, replica), out_shape=jax....]
where the time goes in v2:
time: 35.3 us; the launch traced here: 35.1 us
  Pallas kernels  33.2 us (94%)
  local copies, waits for them, and re-layouts  1.89 us (5%)
    pallas_call x1, Pallas kernels, local(): pl.pallas_call(functools.partial(kernel, tensor, replica), out_shape=jax....  33.2 us
    unnamed x1, local copies, waits for them, and re-layouts  1.89 us

profile of v2, /device:TPU:0, one launch (start us, length us, event | category | flops | bytes accessed | tf_op | source)
XLA Modules:
  0.0 35.1 jit_solution(7574171805808947057)
XLA Ops:
  0.0 33.2 %shard_map.55 = f32[16,64,64]{2,1,0:T(8,128)} custom-call(s32[256]{0:T(256)} %slot_hbm.1, s32[16,16]{1,0:T(8,128)} %cols_hbm.1, s32[256]{0:T(256)} %irreps_hbm.1, bf16[16,64,128]{2,1,0:T(8,128)(2,1)} %amp_hbm.1, bf16[16,8,64,64]{3,2,1,0:T(8,128)(2,1)} %tiles_hbm.1), custom_call_target="tpu_custom_call" | custom-call | flops 134217728 | bytes 4194304 | tf_op jit(solution)/shard_map/pallas_call | solution.py:235
  33.2 1.9 %copy.7 = f32[16,64,64]{2,1,0:T(8,128)} copy(f32[16,64,64]{2,1,0:T(8,128)} %shard_map.55) | data formatting | bytes 524288

commit v3 on v2

--- a/solution.py
+++ b/solution.py
@@ -107,8 +107,8 @@
 
     def visit(action):
         def ring(k, carry):
-            for flow in range(len(flows)):
-                for dx, dy in ((0, 0), (1, 0), (0, 1), (1, 1)):
+            for dx, dy in ((0, 0), (1, 0), (0, 1), (1, 1)):
+                for flow in range(len(flows)):
                     d = k - dx - dy
                     base = t + dx * (1 - 2 * x) + dy * (2 - 4 * y)
                     if dx or dy:
@@ -225,6 +225,7 @@
     def local(amplitudes, block_slot, integrals, tile_cols, irreps):
         blocks, tile, occ = amplitudes.shape
         rows, per_rep = integrals.shape[:2]
+        operands = (block_slot, tile_cols, irreps, amplitudes, integrals)
         wide = max(w for w in (4, 2, 1) if per_rep % w == 0)
         groups = per_rep // wide
         packs = rows // replica
@@ -256,12 +257,12 @@
                 dma((others, packs)),
             ],
             compiler_params=pltpu.CompilerParams(
-                collective_id=0, has_side_effects=True, vmem_limit_bytes=60 << 20
+                collective_id=0, has_side_effects=True, vmem_limit_bytes=48 << 20
             ),
             cost_estimate=pl.CostEstimate(
                 flops=2 * rows * per_rep * tile * tile * occ, bytes_accessed=4 << 20, transcendentals=0
             ),
-        )(block_slot, tile_cols, irreps, amplitudes, integrals)
+        )(*(pltpu.with_memory_space_constraint(v, pltpu.HBM) for v in operands))
 
     in_specs = (
         P("tensor", None, None),

time: 35.3 us -> 32.8 us (0.929)
  Pallas kernels: 33.2 us -> 31.9 us
  local copies, waits for them, and re-layouts: 1.89 us -> 0.8 us
    pallas_call x1, Pallas kernels: 33.2 us -> 31.9 us  [local(): pl.pallas_call(functools.partial(kernel, tensor, replica), out_shape=jax....]
    unnamed x1, local copies, waits for them, and re-layouts: 1.89 us -> 0.8 us
where the time goes in v3:
time: 32.8 us; the launch traced here: 32.7 us
  Pallas kernels  31.9 us (97%)
  local copies, waits for them, and re-layouts  0.8 us (2%)
    pallas_call x1, Pallas kernels, local(): pl.pallas_call(functools.partial(kernel, tensor, replica), out_shape=jax....  31.9 us
    unnamed x1, local copies, waits for them, and re-layouts  0.8 us

profile of v3, /device:TPU:0, one launch (start us, length us, event | category | flops | bytes accessed | tf_op | source)
XLA Modules:
  0.0 32.7 jit_solution(507361514465078695)
XLA Ops:
  0.0 31.9 %shard_map.55 = f32[16,64,64]{2,1,0:T(8,128)S(1)} custom-call(s32[256]{0:T(256)} %slot_hbm.1, s32[16,16]{1,0:T(8,128)} %cols_hbm.1, s32[256]{0:T(256)} %irreps_hbm.1, bf16[16,64,128]{2,1,0:T(8,128)(2,1)} %amp_hbm.1, bf16[16,8,64,64]{3,2,1,0:T(8,128)(2,1)} %tiles_hbm.1), custom_call_target="tpu_custom_call" | custom-call | flops 134217728 | bytes 4194304 | tf_op jit(solution)/shard_map/pallas_call | solution.py:236
  31.9 0.8 %copy.7 = f32[16,64,64]{2,1,0:T(8,128)} copy(f32[16,64,64]{2,1,0:T(8,128)S(1)} %shard_map.55) | data formatting | bytes 524288

commit v4 on v3

--- a/solution.py
+++ b/solution.py
@@ -28,8 +28,8 @@
 def kernel(
     tensor, replica,
     slot_hbm, cols_hbm, irreps_hbm, amp_hbm, tiles_hbm, out_ref,
-    amps, tiles, lhs, index, slot_ref, cols_ref, irreps_ref, outgo, income,
-    local_sem, send_sem, recv_sem, pass_sem, got_sem, sum_send, sum_recv,
+    amps, tiles, lhs, index, slot_ref, cols_ref, irreps_ref,
+    local_sem, send_sem, recv_sem, pass_sem, got_sem, tiles_send, tiles_recv,
 ):
     layers = tensor // 4
     blocks = amp_hbm.shape[0]
@@ -37,7 +37,8 @@
     flows = split(part)
     rows, per_rep = tiles.shape[0], tiles.shape[1]
     width = out_ref.shape[2]
-    groups, wide = lhs.shape[1], per_rep // lhs.shape[1]
+    groups, wide = lhs.shape[2], per_rep // lhs.shape[2]
+    per_row = per_rep * replica
     zero_block = tensor * blocks
     t, r = lax.axis_index("tensor"), lax.axis_index("replica")
     z, y, x = t // 4, (t // 2) % 2, t % 2
@@ -105,7 +106,7 @@
             found += {"x": [X], "y": [Y], "z": [UP, DOWN]}[axis]
         return found
 
-    def visit(action):
+    def visit(action, after=None):
         def ring(k, carry):
             for dx, dy in ((0, 0), (1, 0), (0, 1), (1, 1)):
                 for flow in range(len(flows)):
@@ -116,6 +117,8 @@
                     for dz in (1, -1):
                         inside = (d >= 1) & ((d <= z) if dz > 0 else (d <= layers - 1 - z))
                         action(inside, flow, base - 4 * dz * d, ways(flow, dx, dy, dz))
+            if after is not None:
+                after(k - 1)
             return carry
 
         lax.fori_loop(1, layers + 2, ring, 0)
@@ -132,14 +135,26 @@
 
     def pack(b, carry):
         for g in range(groups):
-            lhs[b, g] = jnp.concatenate([tiles[b, g * wide + i] for i in range(wide)], axis=1)
-        for n in range(per_rep):
-            col = cols_ref[b, r * per_rep + n]
-            same = irreps_ref[col] == irreps_ref[t * rows + b]
-            index[b * per_rep + n] = jnp.where(same, slot_ref[col], zero_block)
+            lhs[r, b, g] = jnp.concatenate([tiles[b, g * wide + i] for i in range(wide)], axis=1)
         return carry
 
     lax.fori_loop(0, rows, pack, 0)
+
+    def share(owner, j):
+        return pltpu.make_async_remote_copy(
+            src_ref=lhs.at[owner], dst_ref=lhs.at[owner],
+            send_sem=tiles_send.at[j - 1], recv_sem=tiles_recv.at[j - 1],
+            device_id={"tensor": t, "replica": (r + j) % replica}, device_id_type=MESH,
+        )
+
+    for j in range(1, replica):
+        share(r, j).start()
+
+    def find(b):
+        mine = irreps_ref[t * rows + b]
+        for n in range(per_row):
+            col = cols_ref[b, n]
+            index[b * per_row + n] = jnp.where(irreps_ref[col] == mine, slot_ref[col], zero_block)
 
     def forward(condition, flow, source, onward):
         @pl.when(condition)
@@ -150,7 +165,14 @@
             for j in range(1, replica):
                 handover(flow, source, j).start()
 
-    visit(forward)
+    share_rows = -(-rows // (layers + 1))
+
+    def find_some(k):
+        lax.fori_loop(
+            jnp.minimum(k * share_rows, rows), jnp.minimum((k + 1) * share_rows, rows), lambda b, _: (find(b), _)[1], 0
+        )
+
+    visit(forward, find_some)
 
     def got(source, carry):
         @pl.when(source != t)
@@ -167,39 +189,18 @@
 
     lax.fori_loop(0, tensor, got, 0)
 
-    packs = rows // replica
-
-    def sums(q, j):
-        return pltpu.make_async_remote_copy(
-            src_ref=outgo.at[j, q], dst_ref=income.at[j - 1, q],
-            send_sem=sum_send.at[j - 1, q], recv_sem=sum_recv.at[j - 1, q],
-            device_id={"tensor": t, "replica": (r + j) % replica}, device_id_type=MESH,
-        )
-
-    for q in range(packs):
-        turned = []
-        for i in range(replica):
-            b = q * replica + i
-            total = None
+    for j in range(1, replica):
+        share((r + replica - j) % replica, j).wait_recv()
+
+    for b in range(rows):
+        total = None
+        for p in range(replica):
             for g in range(groups):
-                rhs = jnp.concatenate(
-                    [amps[index[b * per_rep + g * wide + n]] for n in range(wide)], axis=0
-                )
-                term = jnp.dot(lhs[b, g], rhs, preferred_element_type=jnp.float32)
+                first = b * per_row + p * per_rep + g * wide
+                rhs = jnp.concatenate([amps[index[first + n]] for n in range(wide)], axis=0)
+                term = jnp.dot(lhs[p, b, g], rhs, preferred_element_type=jnp.float32)
                 total = term if total is None else total + term
-            turned.append(pltpu.roll(total, (replica - r) % replica * width, 1))
-        for j in range(replica):
-            outgo[j, q] = jnp.concatenate([v[:, j * width:(j + 1) * width] for v in turned], axis=1)
-        for j in range(1, replica):
-            sums(q, j).start()
-
-    for q in range(packs):
-        total = outgo[0, q]
-        for j in range(1, replica):
-            sums(q, j).wait_recv()
-            total = total + income[j - 1, q]
-        for i in range(replica):
-            out_ref[q * replica + i] = total[:, i * width:(i + 1) * width]
+        out_ref[b] = pltpu.roll(total, (replica - r) % replica * width, 1)[:, :width]
 
     for flow in range(len(flows)):
         for way in ways(flow, 0, 0, 0):
@@ -214,9 +215,8 @@
                 handover(flow, source, j).wait_send()
 
     visit(sent)
-    for q in range(packs):
-        for j in range(1, replica):
-            sums(q, j).wait_send()
+    for j in range(1, replica):
+        share(r, j).wait_send()
 
 
 def solution(mesh):
@@ -228,7 +228,6 @@
         operands = (block_slot, tile_cols, irreps, amplitudes, integrals)
         wide = max(w for w in (4, 2, 1) if per_rep % w == 0)
         groups = per_rep // wide
-        packs = rows // replica
         flows = len(split(blocks // replica))
         hbm = pl.BlockSpec(memory_space=pltpu.HBM)
         dma = pltpu.SemaphoreType.DMA
@@ -241,26 +240,24 @@
             scratch_shapes=[
                 pltpu.VMEM((tensor * blocks + 1, tile, occ), amplitudes.dtype),
                 pltpu.VMEM(integrals.shape, integrals.dtype),
-                pltpu.VMEM((rows, groups, tile, wide * tile), integrals.dtype),
-                pltpu.SMEM((rows * per_rep,), jnp.int32),
+                pltpu.VMEM((replica, rows, groups, tile, wide * tile), integrals.dtype),
+                pltpu.SMEM((rows * per_rep * replica,), jnp.int32),
                 pltpu.SMEM(block_slot.shape, jnp.int32),
                 pltpu.SMEM(tile_cols.shape, jnp.int32),
                 pltpu.SMEM(irreps.shape, jnp.int32),
-                pltpu.VMEM((replica, packs, tile, occ), jnp.float32),
-                pltpu.VMEM((others, packs, tile, occ), jnp.float32),
                 dma((5,)),
                 dma((flows, tensor, 4)),
                 dma((flows, tensor)),
                 dma((others, flows, tensor)),
                 dma((others, flows, tensor)),
-                dma((others, packs)),
-                dma((others, packs)),
+                dma((others,)),
+                dma((others,)),
             ],
             compiler_params=pltpu.CompilerParams(
                 collective_id=0, has_side_effects=True, vmem_limit_bytes=48 << 20
             ),
             cost_estimate=pl.CostEstimate(
-                flops=2 * rows * per_rep * tile * tile * occ, bytes_accessed=4 << 20, transcendentals=0
+                flops=2 * replica * rows * per_rep * tile * tile * occ, bytes_accessed=4 << 20, transcendentals=0
             ),
         )(*(pltpu.with_memory_space_constraint(v, pltpu.HBM) for v in operands))
 

time: 32.8 us -> 29.9 us (0.912)
  the two profiles are of different devices: /device:TPU:0 before, /device:TPU:1 now
where the time goes in v4:
time: 29.9 us; the launch traced here: 29.7 us
  Pallas kernels  28.9 us (97%)
  local copies, waits for them, and re-layouts  0.8 us (3%)
    pallas_call x1, Pallas kernels, local(): pl.pallas_call(functools.partial(kernel, tensor, replica), out_shape=jax....  28.9 us
    unnamed x1, local copies, waits for them, and re-layouts  0.8 us

profile of v4, /device:TPU:1, one launch (start us, length us, event | category | flops | bytes accessed | tf_op | source)
XLA Modules:
  0.0 29.7 jit_solution(11546993260159713722)
XLA Ops:
  0.0 28.9 %shard_map.55 = f32[16,64,64]{2,1,0:T(8,128)S(1)} custom-call(s32[256]{0:T(256)} %slot_hbm.1, s32[16,16]{1,0:T(8,128)} %cols_hbm.1, s32[256]{0:T(256)} %irreps_hbm.1, bf16[16,64,128]{2,1,0:T(8,128)(2,1)} %amp_hbm.1, bf16[16,8,64,64]{3,2,1,0:T(8,128)(2,1)} %tiles_hbm.1), custom_call_target="tpu_custom_call" | custom-call | flops 268435456 | bytes 4194304 | tf_op jit(solution)/shard_map/pallas_call | solution.py:235
  28.9 0.8 %copy.7 = f32[16,64,64]{2,1,0:T(8,128)} copy(f32[16,64,64]{2,1,0:T(8,128)S(1)} %shard_map.55) | data formatting | bytes 524288

commit v5 on v4

--- a/solution.py
+++ b/solution.py
@@ -12,7 +12,7 @@
 
 
 def split(part):
-    plan = (("zyx", 1), ("zxy", 1))
+    plan = (("zyx", 1), ("xzy", 1))
     total = sum(n for _, n in plan)
     if part % total:
         plan, total = (("yzx", 1), ("xzy", 1)), 2
@@ -88,10 +88,11 @@
             device_id={"tensor": jnp.clip(target[way], 0, tensor - 1), "replica": r}, device_id_type=MESH,
         )
 
-    def handover(flow, source, j):
+    def handover(source, owner, j):
+        share_of = amps.at[pl.ds(source * blocks + owner * part, part)]
         return pltpu.make_async_remote_copy(
-            src_ref=place(source, r, flow), dst_ref=place(source, r, flow),
-            send_sem=pass_sem.at[j - 1, flow, source], recv_sem=got_sem.at[j - 1, flow, source],
+            src_ref=share_of, dst_ref=share_of,
+            send_sem=pass_sem.at[j - 1, source], recv_sem=got_sem.at[j - 1, source],
             device_id={"tensor": t, "replica": (r + j) % replica}, device_id_type=MESH,
         )
 
@@ -162,8 +163,9 @@
             hop(flow, source, X).wait_recv()
             for way in onward:
                 when(exists[way], lambda way=way: hop(flow, source, way).start())
-            for j in range(1, replica):
-                handover(flow, source, j).start()
+            if flow == len(flows) - 1:
+                for j in range(1, replica):
+                    handover(source, r, j).start()
 
     share_rows = -(-rows // (layers + 1))
 
@@ -177,14 +179,8 @@
     def got(source, carry):
         @pl.when(source != t)
         def _():
-            for flow in range(len(flows)):
-                for j in range(1, replica):
-                    pltpu.make_async_remote_copy(
-                        src_ref=place(source, (r + replica - j) % replica, flow),
-                        dst_ref=place(source, (r + replica - j) % replica, flow),
-                        send_sem=pass_sem.at[j - 1, flow, source], recv_sem=got_sem.at[j - 1, flow, source],
-                        device_id={"tensor": t, "replica": (r + j) % replica}, device_id_type=MESH,
-                    ).wait_recv()
+            for j in range(1, replica):
+                handover(source, (r + replica - j) % replica, j).wait_recv()
         return carry
 
     lax.fori_loop(0, tensor, got, 0)
@@ -211,8 +207,9 @@
         def _():
             for way in onward:
                 when(exists[way], lambda way=way: hop(flow, source, way).wait_send())
-            for j in range(1, replica):
-                handover(flow, source, j).wait_send()
+            if flow == len(flows) - 1:
+                for j in range(1, replica):
+                    handover(source, r, j).wait_send()
 
     visit(sent)
     for j in range(1, replica):
@@ -248,8 +245,8 @@
                 dma((5,)),
                 dma((flows, tensor, 4)),
                 dma((flows, tensor)),
-                dma((others, flows, tensor)),
-                dma((others, flows, tensor)),
+                dma((others, tensor)),
+                dma((others, tensor)),
                 dma((others,)),
                 dma((others,)),
             ],

time: 29.9 us -> 28.5 us (0.953)
  Pallas kernels: 28.9 us -> 27.5 us
    pallas_call x1, Pallas kernels: 28.9 us -> 27.5 us  [local(): pl.pallas_call(functools.partial(kernel, tensor, replica), out_shape=jax....]
where the time goes in v5:
time: 28.5 us; the launch traced here: 28.3 us
  Pallas kernels  27.5 us (96%)
  local copies, waits for them, and re-layouts  0.8 us (3%)
    pallas_call x1, Pallas kernels, local(): pl.pallas_call(functools.partial(kernel, tensor, replica), out_shape=jax....  27.5 us
    unnamed x1, local copies, waits for them, and re-layouts  0.8 us

profile of v5, /device:TPU:1, one launch (start us, length us, event | category | flops | bytes accessed | tf_op | source)
XLA Modules:
  0.0 28.3 jit_solution(6198079387159392162)
XLA Ops:
  0.0 27.5 %shard_map.55 = f32[16,64,64]{2,1,0:T(8,128)S(1)} custom-call(s32[256]{0:T(256)} %slot_hbm.1, s32[16,16]{1,0:T(8,128)} %cols_hbm.1, s32[256]{0:T(256)} %irreps_hbm.1, bf16[16,64,128]{2,1,0:T(8,128)(2,1)} %amp_hbm.1, bf16[16,8,64,64]{3,2,1,0:T(8,128)(2,1)} %tiles_hbm.1), custom_call_target="tpu_custom_call" | custom-call | flops 268435456 | bytes 4194304 | tf_op jit(solution)/shard_map/pallas_call | solution.py:232
  27.5 0.8 %copy.7 = f32[16,64,64]{2,1,0:T(8,128)} copy(f32[16,64,64]{2,1,0:T(8,128)S(1)} %shard_map.55) | data formatting | bytes 524288
